TPU v7x, 256 devices: a whole 4x4x8 slice. The times are simulated.
256 devices in a mesh: cuts: 4 (over z_hi, core), member: 16 (over y, z_lo), grid: 4 (over x).
Axes of the slice: x: 4, y: 4, z: 8 (z_hi: 2, z_lo: 4; z = z_hi * 4 + z_lo), core: 2. Of those that a mesh axis runs over, the one named last changes fastest.
Arguments:
- hidden: bfloat16 [4, 16, 8192, 1024], P('cuts', 'member', 'grid'), may hold values from -6 to 6
- noise_seeds: int32 [16], P('member'), may hold values from 0 to 63
- noise_table: float32 [64, 1024], replicated, may hold values from -4 to 4
- inner_weight: bfloat16 [1024, 1024], replicated, may hold values from -0.1875 to 0.1875
- inner_bias: float32 [1024], replicated, may hold values from -3 to 3
- output_weight: bfloat16 [100, 1024], replicated, may hold values from -0.1875 to 0.1875
- output_bias: float32 [100], replicated, may hold values from -3 to 3
- state_bank: float32 [8, 100, 4, 16, 128], P(None, None, 'grid', 'member'), may hold values from -6 to 6
- ic_index: int32 [4], P('cuts'), may hold values from 0 to 7
- target_index: int32 [4], P('cuts'), may hold values from 0 to 7
- area_weight: float32 [4, 16, 128], P('grid', 'member'), may hold values from 0.1 to 1
Outputs:
- inner_weight_grad: float32 [1024, 1024], replicated
- inner_bias_grad: float32 [1024], replicated
- output_weight_grad: float32 [100, 1024], replicated
- output_bias_grad: float32 [100], replicated
- loss: float32 [], replicated
All inputs are finite; a program needn't handle non-finite values.
Results may differ from a plain program's by a relative error of at most 0.0037.
Values may be sent and summed in bfloat16 or wider, within the bound.
A program may use at most 128 MiB of HBM per device.

v0:
```python
import jax
import jax.numpy as jnp
from jax import lax
from jax.sharding import PartitionSpec as P

FAIR_ALPHA = 0.95


def body(
    hidden,
    noise_seeds,
    noise_table,
    inner_weight,
    inner_bias,
    output_weight,
    output_bias,
    state_bank,
    ic_index,
    target_index,
    area_weight,
):
    members_here = hidden.shape[1]
    points_here = hidden.shape[2]
    hidden_width = hidden.shape[3]
    variables = output_weight.shape[0]
    seed_ids = jnp.arange(noise_table.shape[0], dtype=jnp.int32)
    seeds_onehot = (noise_seeds[:, None] == seed_ids[None, :]).astype(jnp.float32)
    noise_rows = jnp.dot(
        seeds_onehot,
        noise_table,
        precision=lax.Precision.HIGHEST,
        preferred_element_type=jnp.float32,
    )
    noisy = (hidden[0].astype(jnp.float32) + noise_rows[:, None, :]).astype(jnp.bfloat16)
    noisy = noisy.reshape(members_here * points_here, hidden_width)
    pre_act = jnp.dot(noisy, inner_weight, preferred_element_type=jnp.float32) + inner_bias
    activation, gelu_back = jax.vjp(jax.nn.gelu, pre_act)
    activation = activation.astype(jnp.bfloat16)
    prediction = (
        lax.dot_general(
            output_weight, activation, (((1,), (1,)), ((), ())), preferred_element_type=jnp.float32
        )
        + output_bias[:, None]
    )
    prediction = prediction.reshape(variables, members_here, points_here)
    point_pred = lax.all_to_all(prediction, "member", split_axis=2, concat_axis=1, tiled=True)
    member_count = point_pred.shape[1]
    flat_bank = state_bank[:, :, 0, 0, :]
    ic_state = lax.dynamic_index_in_dim(flat_bank, ic_index[0], 0, keepdims=False)
    truth_field = lax.dynamic_index_in_dim(flat_bank, target_index[0], 0, keepdims=False)
    ensemble = point_pred + ic_state[:, None, :]
    point_weight = area_weight[0, 0]
    sample_count = lax.axis_size("cuts") * hidden.shape[0]
    total_points = lax.axis_size("grid") * points_here
    epsilon = (1.0 - FAIR_ALPHA) / member_count
    pair_scale = (1.0 - epsilon) / (member_count * (member_count - 1.0))
    errors = ensemble - truth_field[:, None, :]
    differences = ensemble[:, :, None, :] - ensemble[:, None, :, :]
    skill_sum = jnp.sum(jnp.abs(errors), axis=1)
    spread_sum = jnp.sum(jnp.abs(differences), axis=(1, 2))
    sign_sums = jnp.sum(jnp.sign(differences), axis=2)
    crps_field = skill_sum / member_count - 0.5 * pair_scale * spread_sum
    local_loss = jnp.sum(point_weight * crps_field) / (sample_count * total_points * variables)
    member_grad = (
        point_weight / sample_count * (jnp.sign(errors) / member_count - pair_scale * sign_sums)
    ).astype(jnp.bfloat16)
    returned = lax.all_to_all(member_grad, "member", split_axis=1, concat_axis=2, tiled=True)
    returned = returned.reshape(variables, members_here * points_here)
    grad_b2 = jnp.sum(returned.astype(jnp.float32), axis=1)
    grad_w2 = jnp.dot(returned, activation, preferred_element_type=jnp.float32)
    carried = lax.dot_general(
        returned, output_weight, (((0,), (0,)), ((), ())), preferred_element_type=jnp.float32
    )
    pre_grad = gelu_back(carried)[0].astype(jnp.bfloat16)
    grad_b1 = jnp.sum(pre_grad.astype(jnp.float32), axis=0)
    grad_w1 = lax.dot_general(
        noisy, pre_grad, (((0,), (0,)), ((), ())), preferred_element_type=jnp.float32
    )
    grad_w1, grad_b1, grad_w2, grad_b2, loss = lax.psum(
        (grad_w1, grad_b1, grad_w2, grad_b2, local_loss), ("cuts", "member", "grid")
    )
    return (grad_w1, grad_b1, grad_w2, grad_b2, loss)


def solution(mesh):
    return jax.shard_map(
        body,
        mesh=mesh,
        in_specs=(
            P("cuts", "member", "grid", None),
            P("member"),
            P(),
            P(),
            P(),
            P(),
            P(),
            P(None, None, "grid", "member", None),
            P("cuts"),
            P("cuts"),
            P("grid", "member", None),
        ),
        out_specs=(P(), P(), P(), P(), P()),
        check_vma=False,
    )
```

profile of v0, /device:TPU:97, one launch (start us, length us, event | category | flops | bytes accessed | tf_op | source)
XLA Modules:
  0.0 390.6 jit_solution(8578856110412567470)
XLA Ops:
  7.2 0.0 copy-start
  8.0 1.2 fusion.15
  9.1 0.0 copy-done
  9.1 0.0 copy-start.4
  9.1 0.0 copy-start.5
  9.2 11.4 %multiply_convert_fusion = (bf16[2048,1024]{1,0:T(8,128)(2,1)S(1)}, f32[2048,1024]{1,0:T(8,128)}) fusion(f32[1024]{0:T(1024)} %param.15, bf16[1024,1024]{1,0:T(8,128)(2,1)S(1)} %copy-done, bf16[1,1,2048,1024]{3,2,1,0:T(8,128)(2,1)} %param.11, f32[1024]{0:T(1024)S(1)} %bitcast.54), kind=kOutput, calls=%fused_computation.16 | convolution fusion | flops 4322230272 | bytes 18882560 | tf_op jit(solution)/shard_map/dot_general | solution.py:36
  20.6 0.0 copy-start.1
  20.6 0.0 copy-start.6
  20.6 2.0 copy-done.1
  22.6 0.0 copy-done.4
  22.6 0.0 copy-done.5
  22.6 1.4 fusion.14
  24.1 1.9 copy.23
  26.0 7.2 %all-to-all-start = ((f32[100,1,2048]{0,1,2:T(1,128)}), f32[100,1,2048]{0,1,2:T(1,128)S(1)}, u32[]{:S(2)}, u32[]{:S(2)}) async-start(f32[100,1,2048]{0,1,2:T(1,128)} %copy.23), calls=%async_computation | async-start | bytes 2097152 | tf_op jit(solution)/shard_map/all_to_all | solution.py:46
  33.2 0.2 all-reduce.4.cloned.1.call-start
  34.7 0.9 constant_dynamic-slice_fusion.1
  35.6 0.0 copy-done.6
  35.6 21.7 %all-to-all-done = f32[100,1,2048]{0,1,2:T(1,128)S(1)} async-done(((f32[100,1,2048]{0,1,2:T(1,128)}), f32[100,1,2048]{0,1,2:T(1,128)S(1)}, u32[]{:S(2)}, u32[]{:S(2)}) %all-to-all-start) | async-done | bytes 819232 | tf_op jit(solution)/shard_map/all_to_all | solution.py:46
  57.3 0.0 copy-start.8
  57.3 1.4 copy.27
  58.7 0.0 copy-start.2
  58.7 1.6 abs_reduce_fusion
  60.3 7.5 %fusion.1 = (f32[100,128]{1,0:T(8,128)S(1)}, f32[100,16,128]{2,1,0:T(8,128)S(1)}) fusion(f32[100,16,128]{2,1,0:T(8,128)S(1)} %get-tuple-element.13), kind=kLoop, calls=%fused_computation.3 | loop fusion | flops 16166400 | bytes 1689600 | tf_op jit(solution)/shard_map/reduce_sum | solution.py:60
  67.8 0.4 multiply_convert_fusion.1
  68.2 0.1 copy.25
  68.3 17.2 %all_to_all.21 = bf16[100,16,128]{2,0,1:T(8,128)(2,1)S(1)} all-to-all(bf16[100,16,128]{2,0,1:T(8,128)(2,1)S(1)} %copy.25), channel_id=1, replica_groups=mesh['cuts'=4,'member'=16,'grid'=4] {'member'}, dimensions={1} | all-to-all | bytes 819200 | tf_op jit(solution)/shard_map/all_to_all | solution.py:67
  85.5 0.1 copy.26
  85.6 0.1 copy.30
  85.7 0.0 copy-done.2
  85.7 1.5 fusion.20
  87.2 0.0 copy-done.8
  87.2 0.0 copy-start.7
  87.2 9.0 %convert_reduce_fusion = (f32[1024]{0:T(1024)S(1)}, bf16[2048,1024]{1,0:T(8,128)(2,1)S(1)}) fusion(f32[2048,1024]{1,0:T(8,128)} %get-tuple-element.17, f32[1024]{0:T(1024)S(1)} %copy-done.8, bf16[100,2048]{1,0:T(8,128)(2,1)S(1)} %bitcast.49, bf16[100,1024]{1,0:T(8,128)(2,1)S(1)} %copy-done.4), kind=kOutput, calls=%fused_computation.15 | convolution fusion | flops 467663872 | bytes 13205504 | tf_op jit(solution)/shard_map/dot_general | solution.py:71
  96.2 0.0 copy-done.7
  96.2 6.1 %fusion.10 = f32[1024,1024]{1,0:T(8,128)} fusion(bf16[2048,1024]{1,0:T(8,128)(2,1)S(1)} %get-tuple-element.19, bf16[1,1,2048,1024]{3,2,1,0:T(8,128)(2,1)S(1)} %copy-done.7, f32[1024]{0:T(1024)S(1)} %bitcast.55), kind=kOutput, calls=%fused_computation.17 | convolution fusion | flops 4301258752 | bytes 12587008 | tf_op jit(solution)/shard_map/dot_general | solution.py:76
  102.3 0.0 all-reduce.4.cloned.1.call-update
  102.3 0.6 multiply_reduce_fusion
  103.6 0.1 convert_reduce_fusion.1
  103.7 79.0 %all-reduce = (f32[1024]{0:T(1024)}, f32[100]{0:T(128)}, f32[]{:T(128)}) all-reduce(f32[1024]{0:T(1024)S(1)} %get-tuple-element.18, f32[100]{0:T(128)S(1)} %convert_reduce_fusion.1, f32[]{:T(128)S(6)} %div.27), channel_id=1, replica_groups=mesh['cuts'=4,'member'=16,'grid'=4] {'cuts','member','grid'}, use_global_device_ids=true, to_apply=%region_3.4 | all-reduce | flops 1125 | bytes 9000 | tf_op jit(solution)/shard_map/psum | solution.py:79
  182.7 195.4 %all-reduce.4.cloned.1.call-done = (f32[1024,1024]{1,0:T(8,128)}, f32[100,1024]{1,0:T(8,128)}) async-done(((f32[1024,1024]{1,0:T(8,128)}, f32[100,1024]{1,0:T(8,128)}), (f32[1024,1024]{1,0:T(8,128)}, f32[100,1024]{1,0:T(8,128)})) %all-reduce.4.cloned.1.call-update) | async-done | bytes 4603920 | tf_op jit(solution)/shard_map/psum | solution.py:79
  378.2 0.0 copy-start.3
  378.2 4.8 %copy.40 = f32[1024,1024]{1,0:T(8,128)} copy(f32[1024,1024]{1,0:T(8,128)} %get-tuple-element.20) | data formatting | bytes 8388608
  383.0 0.0 copy-done.3
  383.0 0.8 copy.41
  (4 shorter events, 0.0 us)
Async XLA Ops:
  7.2 2.0 copy-start
  9.1 13.5 %copy-start.4 = (bf16[100,1024]{1,0:T(8,128)(2,1)S(1)}, bf16[100,1024]{1,0:T(8,128)(2,1)}, u32[]{:S(2)}) copy-start(bf16[100,1024]{1,0:T(8,128)(2,1)} %param.16) | copy-start | bytes 614404
  9.1 13.5 %copy-start.5 = (f32[100]{0:T(128)S(1)}, f32[100]{0:T(128)}, u32[]{:S(2)}) copy-start(f32[100]{0:T(128)} %param.17) | copy-start | bytes 1204
  20.6 2.0 copy-start.1
  20.6 15.0 %copy-start.6 = (f32[1,1,128]{2,1,0:T(1,128)S(1)}, f32[1,1,128]{2,1,0:T(1,128)}, u32[]{:S(2)}) copy-start(f32[1,1,128]{2,1,0:T(1,128)} %param.21) | copy-start | bytes 1540
  26.0 31.4 %all-to-all-start = ((f32[100,1,2048]{0,1,2:T(1,128)}), f32[100,1,2048]{0,1,2:T(1,128)S(1)}, u32[]{:S(2)}, u32[]{:S(2)}) async-start(f32[100,1,2048]{0,1,2:T(1,128)} %copy.23), calls=%async_computation | async-start | bytes 2097152 | tf_op jit(solution)/shard_map/all_to_all | solution.py:46
  33.2 345.0 %all-reduce.4.cloned.1.call-start = ((), (), s32[]{:S(2)}) async-start(), calls=%async_computation.2 | async-start | bytes 9240576 | tf_op jit(solution)/shard_map/psum | solution.py:79
  57.3 29.9 %copy-start.8 = (f32[1024]{0:T(1024)S(1)}, f32[1024]{0:T(1024)}, u32[]{:S(2)}) copy-start(f32[1024]{0:T(1024)} %param.15) | copy-start | bytes 12292
  58.7 27.0 %copy-start.2 = (bf16[2048,1024]{1,0:T(8,128)(2,1)S(1)}, bf16[2048,1024]{1,0:T(8,128)(2,1)}, u32[]{:S(2)}) copy-start(bf16[2048,1024]{1,0:T(8,128)(2,1)} %copy-done.1) | copy-start | bytes 12582916
  87.2 9.0 %copy-start.7 = (bf16[1,1,2048,1024]{3,2,1,0:T(8,128)(2,1)S(1)}, bf16[1,1,2048,1024]{3,2,1,0:T(8,128)(2,1)}, u32[]{:S(2)}) copy-start(bf16[1,1,2048,1024]{3,2,1,0:T(8,128)(2,1)} %param.11) | copy-start | bytes 12582916
  378.2 4.8 %copy-start.3 = (f32[100,1024]{1,0:T(8,128)S(1)}, f32[100,1024]{1,0:T(8,128)}, u32[]{:S(2)}) copy-start(f32[100,1024]{1,0:T(8,128)} %get-tuple-element.22) | copy-start | bytes 1228804
Sparse Core Ops, SparseCore 0:
  102.4 275.6 all-reduce.3
where the time goes:
time: 391 us
  waiting for transfers between devices  217 us (55%)
  blocking collectives  96.2 us (25%)
  matrix products  30.6 us (8%)
  between operations  16.9 us (4%)
  local copies, waits for them, and re-layouts  12.1 us (3%)
  other arithmetic  10.2 us (3%)
  starting transfers between devices  7.4 us (2%)
    psum x1, waiting for transfers between devices, body(): lax.psum((grad_w1, grad_b1, grad_w2, grad_b2, local_loss), ('cuts', 'memb...  195 us
    psum x1, blocking collectives, body(): lax.psum((grad_w1, grad_b1, grad_w2, grad_b2, local_loss), ('cuts', 'memb...  79 us
    all_to_all x1, waiting for transfers between devices, body(): lax.all_to_all(prediction, 'member', split_axis=2, concat_axis=1, tiled=T...  21.7 us
    all_to_all x1, blocking collectives, body(): lax.all_to_all(member_grad, 'member', split_axis=1, concat_axis=2, tiled=...  17.2 us
    dot_general x1, matrix products, body(): jnp.dot(noisy, inner_weight, preferred_element_type=jnp.float32)  11.4 us
    dot_general x1, matrix products, body(): lax.dot_general(returned, output_weight, (((0,), (0,)), ((), ())), prefer...  8.97 us
  transfers between devices with their start and end apart: 2, of which 2 were waited for; matrix products, arithmetic and copies ran while one was open for 0% of the time, Pallas kernels for 0%

commit v1 on v0

--- a/solution.py
+++ b/solution.py
@@ -4,6 +4,12 @@
 from jax.sharding import PartitionSpec as P
 
 FAIR_ALPHA = 0.95
+
+
+def get_boxes_in(mesh_dim, ax_name, local_array):
+    for w in (mesh_dim, ax_name):
+        local_array = lax.psum(local_array, w)
+    return local_array
 
 
 def body(
@@ -76,8 +82,8 @@
     grad_w1 = lax.dot_general(
         noisy, pre_grad, (((0,), (0,)), ((), ())), preferred_element_type=jnp.float32
     )
-    grad_w1, grad_b1, grad_w2, grad_b2, loss = lax.psum(
-        (grad_w1, grad_b1, grad_w2, grad_b2, local_loss), ("cuts", "member", "grid")
+    grad_w1, grad_b1, grad_w2, grad_b2, loss = get_boxes_in(
+        ("member", "grid"), "cuts", local_array=(grad_w1, grad_b1, grad_w2, grad_b2, local_loss)
     )
     return (grad_w1, grad_b1, grad_w2, grad_b2, loss)
 

time: 391 us -> 1080 us (2.76)
  waiting for transfers between devices: 217 us -> 682 us
  blocking collectives: 96.2 us -> 313 us
    psum x1 -> x2, waiting for transfers between devices: 195 us -> 660 us  [get_boxes_in(): local_array = lax.psum(local_array, w)]
    psum x1 -> x2, blocking collectives: 79 us -> 295 us  [get_boxes_in(): local_array = lax.psum(local_array, w)]
  transfers between devices with their start and end apart: 2 -> 3, of which waited for: 2 -> 2; matrix products, arithmetic and copies ran while one was open for 0% -> 0% of each run, Pallas kernels for 0% -> 0%
where the time goes in v1:
time: 1080 us; the launch traced here: 1070 us
  waiting for transfers between devices  682 us (63%)
  blocking collectives  313 us (29%)
  matrix products  30.6 us (3%)
  between operations  16.9 us (2%)
  local copies, waits for them, and re-layouts  12.1 us (1%)
    psum x2, waiting for transfers between devices, get_boxes_in(): local_array = lax.psum(local_array, w)  660 us
    psum x2, blocking collectives, get_boxes_in(): local_array = lax.psum(local_array, w)  295 us
    all_to_all x1, waiting for transfers between devices, body(): lax.all_to_all(prediction, 'member', split_axis=2, concat_axis=1, tiled=T...  21.7 us
  transfers between devices with their start and end apart: 3, of which 2 were waited for; matrix products, arithmetic and copies ran while one was open for 0% of the time, Pallas kernels for 0%

profile of v1, /device:TPU:97, one launch (start us, length us, event | category | flops | bytes accessed | tf_op | source)
XLA Modules:
  0.0 1072.1 jit_solution(4926426083944261445)
XLA Ops:
  7.2 0.0 copy-start
  8.0 1.2 fusion.15
  9.1 0.0 copy-done
  9.1 0.0 copy-start.4
  9.1 0.0 copy-start.5
  9.2 11.4 %multiply_convert_fusion = (bf16[2048,1024]{1,0:T(8,128)(2,1)S(1)}, f32[2048,1024]{1,0:T(8,128)}) fusion(f32[1024]{0:T(1024)} %param.15, bf16[1024,1024]{1,0:T(8,128)(2,1)S(1)} %copy-done, bf16[1,1,2048,1024]{3,2,1,0:T(8,128)(2,1)} %param.11, f32[1024]{0:T(1024)S(1)} %bitcast.54), kind=kOutput, calls=%fused_computation.16 | convolution fusion | flops 4322230272 | bytes 18882560 | tf_op jit(solution)/shard_map/dot_general | solution.py:42
  20.6 0.0 copy-start.1
  20.6 0.0 copy-start.6
  20.6 2.0 copy-done.1
  22.6 0.0 copy-done.4
  22.6 0.0 copy-done.5
  22.6 1.4 fusion.14
  24.1 1.9 copy.23
  26.0 7.2 all-to-all-start
  33.2 0.2 all-reduce.7.cloned.1.call-start
  34.7 0.9 constant_dynamic-slice_fusion.1
  35.6 0.0 copy-done.6
  35.6 21.7 %all-to-all-done = f32[100,1,2048]{0,1,2:T(1,128)S(1)} async-done(((f32[100,1,2048]{0,1,2:T(1,128)}), f32[100,1,2048]{0,1,2:T(1,128)S(1)}, u32[]{:S(2)}, u32[]{:S(2)}) %all-to-all-start) | async-done | bytes 819232 | tf_op jit(solution)/shard_map/all_to_all | solution.py:52
  57.3 0.0 copy-start.8
  57.3 1.4 copy.27
  58.7 0.0 copy-start.2
  58.7 1.6 abs_reduce_fusion
  60.3 7.5 fusion.1
  67.8 0.4 multiply_convert_fusion.1
  68.2 0.1 copy.25
  68.3 17.2 %all_to_all.21 = bf16[100,16,128]{2,0,1:T(8,128)(2,1)S(1)} all-to-all(bf16[100,16,128]{2,0,1:T(8,128)(2,1)S(1)} %copy.25), channel_id=1, replica_groups=mesh['cuts'=4,'member'=16,'grid'=4] {'member'}, dimensions={1} | all-to-all | bytes 819200 | tf_op jit(solution)/shard_map/all_to_all | solution.py:73
  85.5 0.1 copy.26
  85.6 0.1 copy.30
  85.7 0.0 copy-done.2
  85.7 1.5 fusion.20
  87.2 0.0 copy-done.8
  87.2 0.0 copy-start.7
  87.2 9.0 convert_reduce_fusion
  96.2 0.0 copy-done.7
  96.2 6.1 fusion.10
  102.3 0.0 all-reduce.7.cloned.1.call-update
  102.3 0.0 all-reduce.9.cloned.1.call-start
  102.4 660.4 %all-reduce.7.cloned.1.call-done = (f32[1024,1024]{1,0:T(8,128)}, f32[100,1024]{1,0:T(8,128)}) async-done(((f32[1024,1024]{1,0:T(8,128)}, f32[100,1024]{1,0:T(8,128)}), (f32[1024,1024]{1,0:T(8,128)}, f32[100,1024]{1,0:T(8,128)})) %all-reduce.7.cloned.1.call-update) | async-done | bytes 4603920 | tf_op jit(solution)/shard_map/psum | solution.py:11
  762.8 0.0 all-reduce.9.cloned.1.call-update
  762.8 0.6 multiply_reduce_fusion
  764.1 0.1 convert_reduce_fusion.1
  764.2 182.3 %all-reduce = (f32[1024]{0:T(1024)S(1)}, f32[100]{0:T(128)S(1)}, f32[]{:T(128)}) all-reduce(f32[1024]{0:T(1024)S(1)} %get-tuple-element.23, f32[100]{0:T(128)S(1)} %convert_reduce_fusion.1, f32[]{:T(128)S(6)} %div.27), channel_id=1, replica_groups=mesh['cuts'=4,'member'=16,'grid'=4] {'member','grid'}, use_global_device_ids=true, to_apply=%region_4.5 | all-reduce | flops 1125 | bytes 9000 | tf_op jit(solution)/shard_map/psum | solution.py:11
  946.5 113.2 %all-reduce.2 = (f32[1024]{0:T(1024)}, f32[100]{0:T(128)}, f32[]{:T(128)}) all-reduce(f32[1024]{0:T(1024)S(1)} %get-tuple-element.7, f32[100]{0:T(128)S(1)} %get-tuple-element.8, f32[]{:T(128)} %get-tuple-element.9), channel_id=1, replica_groups=mesh['cuts'=4,'member'=16,'grid'=4] {'cuts'}, use_global_device_ids=true, to_apply=%region_5.6 | all-reduce | flops 1125 | bytes 9000 | tf_op jit(solution)/shard_map/psum | solution.py:11
  1059.7 0.0 all-reduce.9.cloned.1.call-done
  1059.7 0.0 copy-start.3
  1059.7 4.8 copy.42
  1064.5 0.0 copy-done.3
  1064.5 0.8 copy.43
  (4 shorter events, 0.0 us)
Async XLA Ops:
  7.2 2.0 copy-start
  9.1 13.5 %copy-start.4 = (bf16[100,1024]{1,0:T(8,128)(2,1)S(1)}, bf16[100,1024]{1,0:T(8,128)(2,1)}, u32[]{:S(2)}) copy-start(bf16[100,1024]{1,0:T(8,128)(2,1)} %param.16) | copy-start | bytes 614404
  9.1 13.5 %copy-start.5 = (f32[100]{0:T(128)S(1)}, f32[100]{0:T(128)}, u32[]{:S(2)}) copy-start(f32[100]{0:T(128)} %param.17) | copy-start | bytes 1204
  20.6 2.0 copy-start.1
  20.6 15.0 %copy-start.6 = (f32[1,1,128]{2,1,0:T(1,128)S(1)}, f32[1,1,128]{2,1,0:T(1,128)}, u32[]{:S(2)}) copy-start(f32[1,1,128]{2,1,0:T(1,128)} %param.21) | copy-start | bytes 1540
  26.0 31.4 %all-to-all-start = ((f32[100,1,2048]{0,1,2:T(1,128)}), f32[100,1,2048]{0,1,2:T(1,128)S(1)}, u32[]{:S(2)}, u32[]{:S(2)}) async-start(f32[100,1,2048]{0,1,2:T(1,128)} %copy.23), calls=%async_computation | async-start | bytes 2097152 | tf_op jit(solution)/shard_map/all_to_all | solution.py:52
  33.2 729.6 %all-reduce.7.cloned.1.call-start = ((), (), s32[]{:S(2)}) async-start(), calls=%async_computation.2 | async-start | bytes 9240576 | tf_op jit(solution)/shard_map/psum | solution.py:11
  57.3 29.9 %copy-start.8 = (f32[1024]{0:T(1024)S(1)}, f32[1024]{0:T(1024)}, u32[]{:S(2)}) copy-start(f32[1024]{0:T(1024)} %param.15) | copy-start | bytes 12292
  58.7 27.0 %copy-start.2 = (bf16[2048,1024]{1,0:T(8,128)(2,1)S(1)}, bf16[2048,1024]{1,0:T(8,128)(2,1)}, u32[]{:S(2)}) copy-start(bf16[2048,1024]{1,0:T(8,128)(2,1)} %copy-done.1) | copy-start | bytes 12582916
  87.2 9.0 copy-start.7
  102.3 957.4 %all-reduce.9.cloned.1.call-start = ((), (), s32[]{:S(2)}) async-start(), calls=%async_computation.3 | async-start | bytes 9240576 | tf_op jit(solution)/shard_map/psum | solution.py:11
  1059.7 4.8 copy-start.3
Sparse Core Ops, SparseCore 0:
  102.4 660.2 all-reduce.6
  765.5 241.1 all-reduce.8
